TPU v7x, 512 devices: a whole 4x4x16 slice. The times are simulated.
512 devices in a mesh: gx: 8 (over z_lo), gy: 8 (over y, z_hi), gz: 8 (over x, core).
Axes of the slice: x: 4, y: 4, z: 16 (z_hi: 2, z_lo: 8; z = z_hi * 8 + z_lo), core: 2. Of those that a mesh axis runs over, the one named last changes fastest.
Arguments:
- hidden_pre: bfloat16 [2048, 24576], P('gy', ('gz', 'gx')), may hold values from -6 to 6
- grad_out: bfloat16 [2048, 12288], P(('gx', 'gz'), 'gy'), may hold values from -16 to 16
- down_weight: bfloat16 [24576, 12288], P(('gz', 'gx'), 'gy'), may hold values from -0.0546875 to 0.0546875
Outputs:
- grad_hidden: bfloat16 [2048, 24576], P('gy', ('gz', 'gx'))
- grad_weight: float32 [24576, 12288], P(('gz', 'gx'), 'gy')
All inputs are finite; a program needn't handle non-finite values.
Results may differ from a plain program's by a relative error of at most 0.0029.
Values may be sent and summed in bfloat16 or wider, within the bound.
A program may use at most 64 MiB of HBM per device.

v0:
```python
import math

import jax
import jax.numpy as jnp
from jax import lax
from jax.sharding import PartitionSpec as P

coeff = math.sqrt(2.0 / math.pi)


def gelu_value(h):
    inner = coeff * (h + 0.044715 * h * h * h)
    return 0.5 * h * (1.0 + jnp.tanh(inner))


def gelu_slope(h):
    inner = coeff * (h + 0.044715 * h * h * h)
    tval = jnp.tanh(inner)
    return 0.5 * (1.0 + tval) + 0.5 * h * (1.0 - tval * tval) * coeff * (
        1.0 + 3.0 * 0.044715 * h * h
    )


def against_weight(rows, down_weight):
    return lax.dot_general(
        rows, down_weight, (((1,), (1,)), ((), ())), preferred_element_type=jnp.float32
    )


def token_sum(left, right):
    return lax.dot_general(
        left, right, (((0,), (0,)), ((), ())), preferred_element_type=jnp.float32
    )


def body(hidden_pre, grad_out, down_weight):
    hfull = hidden_pre.astype(jnp.float32)
    act = gelu_value(hfull).astype(jnp.bfloat16)
    act_all = lax.all_gather(act, "gy", axis=0, tiled=True)
    rows_all = lax.all_gather(grad_out, ("gx", "gz"), axis=0, tiled=True)
    grad_act = lax.psum_scatter(
        against_weight(rows_all, down_weight), "gy", scatter_dimension=0, tiled=True
    )
    grad_weight = token_sum(act_all, rows_all)
    grad_hidden = (grad_act * gelu_slope(hfull)).astype(jnp.bfloat16)
    return (grad_hidden, grad_weight)


def solution(mesh):
    placed = (P("gy", ("gz", "gx")), P(("gx", "gz"), "gy"), P(("gz", "gx"), "gy"))
    return jax.shard_map(
        body,
        mesh=mesh,
        in_specs=placed,
        out_specs=(P("gy", ("gz", "gx")), P(("gz", "gx"), "gy")),
        check_vma=False,
    )
```

profile of v0, /device:TPU:1, one launch (start us, length us, event | category | flops | bytes accessed | tf_op | source)
XLA Modules:
  0.0 435.6 jit_solution(5150176140271094762)
XLA Ops:
  7.2 0.0 copy-start
  7.2 0.0 all-gather.3.cloned.1.call-start
  7.2 0.7 all-gather.3.cloned.1.call-update
  7.9 0.0 reduce-scatter.2.cloned.1.call-start
  8.0 133.6 %all-gather.3.cloned.1.call-done = bf16[2048,1536]{1,0:T(8,128)(2,1)} async-done(((bf16[32,1536]{1,0:T(8,128)(2,1)}), bf16[2048,1536]{1,0:T(8,128)(2,1)}) %all-gather.3.cloned.1.call-update) | async-done | bytes 6291472 | tf_op jit(solution)/shard_map/all_gather | solution.py:40
  141.5 0.0 copy-done
  141.5 7.9 %fusion.11 = f32[2048,384]{1,0:T(8,128)} fusion(bf16[2048,1536]{1,0:T(8,128)(2,1)} %all-gather.3.cloned.1.call-done, bf16[384,1536]{1,0:T(8,128)(2,1)S(1)} %copy-done), kind=kOutput, calls=%fused_computation.18 | convolution fusion | flops 2415919104 | bytes 10616832 | tf_op jit(solution)/shard_map/dot_general | solution.py:25
  149.5 0.0 copy-start.1
  149.5 0.0 reduce-scatter.2.cloned.1.call-update
  149.5 0.0 all-gather.5.cloned.1.call-start
  149.6 171.7 %reduce-scatter.2.cloned.1.call-done = f32[256,384]{1,0:T(8,128)} async-done(((f32[2048,384]{1,0:T(8,128)}), f32[256,384]{1,0:T(8,128)}) %reduce-scatter.2.cloned.1.call-update) | async-done | bytes 393232 | tf_op jit(solution)/shard_map/reduce_scatter | solution.py:41
  321.2 0.0 copy-done.1
  321.2 2.0 fusion.7
  323.3 0.0 all-gather.5.cloned.1.call-update
  323.3 98.4 %all-gather.5.cloned.1.call-done = bf16[2048,384]{1,0:T(8,128)(2,1)} async-done(((bf16[256,384]{1,0:T(8,128)(2,1)}), bf16[2048,384]{1,0:T(8,128)(2,1)}) %all-gather.5.cloned.1.call-update) | async-done | bytes 1572880 | tf_op jit(solution)/shard_map/all_gather | solution.py:39
  421.7 7.3 %fusion.12 = f32[384,1536]{1,0:T(8,128)} fusion(bf16[2048,384]{1,0:T(8,128)(2,1)} %all-gather.5.cloned.1.call-done, bf16[2048,1536]{1,0:T(8,128)(2,1)} %all-gather.3.cloned.1.call-done), kind=kOutput, calls=%fused_computation.19 | convolution fusion | flops 2415919104 | bytes 10223616 | tf_op jit(solution)/shard_map/dot_general | solution.py:31
Async XLA Ops:
  7.2 134.4 %copy-start = (bf16[384,1536]{1,0:T(8,128)(2,1)S(1)}, bf16[384,1536]{1,0:T(8,128)(2,1)}, u32[]{:S(2)}) copy-start(bf16[384,1536]{1,0:T(8,128)(2,1)} %param.5) | copy-start | bytes 3538948
  7.2 134.4 %all-gather.3.cloned.1.call-start = ((), (), s32[]{:S(2)}) async-start(), calls=%async_computation.1 | async-start | bytes 6389760 | tf_op jit(solution)/shard_map/all_gather | solution.py:40
  7.9 313.3 %reduce-scatter.2.cloned.1.call-start = ((), (), s32[]{:S(2)}) async-start(), calls=%async_computation.2 | async-start | bytes 3538944 | tf_op jit(solution)/shard_map/reduce_scatter | solution.py:41
  149.5 171.8 %copy-start.1 = (bf16[256,384]{1,0:T(8,128)(2,1)S(1)}, bf16[256,384]{1,0:T(8,128)(2,1)}, u32[]{:S(2)}) copy-start(bf16[256,384]{1,0:T(8,128)(2,1)} %param.3) | copy-start | bytes 589828
  149.5 272.2 %all-gather.5.cloned.1.call-start = ((), (), s32[]{:S(2)}) async-start(), calls=%async_computation.3 | async-start | bytes 1769472 | tf_op jit(solution)/shard_map/all_gather | solution.py:39
Sparse Core Ops, SparseCore 0:
  10.2 131.3 all-gather.2
  149.6 171.5 reduce-scatter.1
  325.5 96.1 all-gather.4
where the time goes:
time: 436 us
  waiting for transfers between devices  404 us (93%)
  matrix products  15.3 us (4%)
  between operations  13.8 us (3%)
    reduce_scatter x1, waiting for transfers between devices, body(): lax.psum_scatter(against_weight(rows_all, down_weight), 'gy', scatter_dim...  172 us
    all_gather x1, waiting for transfers between devices, body(): rows_all = lax.all_gather(grad_out, ('gx', 'gz'), axis=0, tiled=True)  134 us
    all_gather x1, waiting for transfers between devices, body(): act_all = lax.all_gather(act, 'gy', axis=0, tiled=True)  98.4 us
  transfers between devices with their start and end apart: 3, of which 3 were waited for; matrix products, arithmetic and copies ran while one was open for 0% of the time, Pallas kernels for 0%

commit v1 on v0

v1 whole, which is shorter than its diff:
```python
import math

import jax
import jax.numpy as jnp
from jax import lax
from jax.experimental import pallas as pl
from jax.experimental.pallas import tpu as pltpu
from jax.sharding import PartitionSpec as P

MESH = pl.DeviceIdType.MESH
coeff = math.sqrt(2.0 / math.pi)

NZ, NY, NX = 8, 4, 4
BLK = 32
TOK = 256
QTR = TOK // NY
FEAT = 1536
HID = 384
TILE = 256
NT = FEAT // TILE
ACT_SEND, ACT_PASS = 3, 10
LAST = 13


def kernel(h_ref, g_ref, w_hbm, gh_ref, dw_hbm,
           rows_all, w_ref, act_t, slope, part, from_y, kept, z_out, z_in, full, dw_buf,
           w_sem, dw_sem, zs, zr, xs, xr, hs, hr, cs, cr, ys, yr, ts, tr, as_, ar, fs, fr):
    gx, gy, gz = lax.axis_index("gx"), lax.axis_index("gy"), lax.axis_index("gz")
    y, zh = gy // 2, gy % 2
    x, c = gz // 2, gz % 2
    z = gx

    def at_z(v):
        return {"gx": v, "gy": gy, "gz": gz}

    def at_x(o):
        return {"gx": gx, "gy": gy, "gz": ((x + o) % NX) * 2 + c}

    def at_y(v):
        return {"gx": gx, "gy": v * 2 + zh, "gz": gz}

    twin = {"gx": gx, "gy": gy, "gz": x * 2 + (1 - c)}
    far = {"gx": gx, "gy": y * 2 + (1 - zh), "gz": gz}

    def block(j, xx, cc, start=0, size=BLK):
        return rows_all.at[pl.ds(pl.multiple_of(((j * NX + xx) * 2 + cc) * BLK + start, 16), size)]

    def remote(src, dst, send, recv, to):
        return pltpu.make_async_remote_copy(
            src_ref=src, dst_ref=dst, send_sem=send, recv_sem=recv, device_id=to, device_id_type=MESH)

    def z_copy(j, up):
        b = block(j, x, c)
        return remote(b, b, zs.at[up, j], zr.at[j], at_z(z + 1 if up else z - 1))

    def x_copy(j, up):
        b = block(j, x, c)
        return remote(b, b, xs.at[up, j], xr.at[up, j], at_x(1 if up else -1))

    def x_came(j, up):
        b = block(j, (x + (NX - 1 if up else 1)) % NX, c)
        return remote(b, b, xs.at[up, j], xr.at[up, j], at_x(1 if up else -1))

    def half_copy(j, up):
        b = block(j, (x + (NX - 1 if up else 1)) % NX, c, 0 if up else 16, 16)
        return remote(b, b, hs.at[up, j], hr.at[up, j], at_x(1 if up else -1))

    def half_came(j, up):
        b = block(j, (x + 2) % NX, c, 0 if up else 16, 16)
        return remote(b, b, hs.at[up, j], hr.at[up, j], at_x(1 if up else -1))

    def c_copy(j, o):
        b = block(j, (x + o) % NX, c)
        return remote(b, b, cs.at[o, j], cr.at[o, j], twin)

    def c_came(j, o):
        b = block(j, (x + o) % NX, 1 - c)
        return remote(b, b, cs.at[o, j], cr.at[o, j], twin)

    def y_copy(j, o):
        yt = (y + o) % NY
        return remote(part.at[j, pl.ds(pl.multiple_of(yt * QTR, QTR), QTR)], from_y.at[o - 1, j],
                      ys.at[o - 1, j], yr.at[o - 1, j], at_y(yt))

    def far_copy(k):
        return remote(z_out.at[k], z_in.at[k], ts.at[k], tr.at[k], far)

    def full_copy(k):
        return remote(kept.at[k], full.at[pl.ds(pl.multiple_of(y * QTR, QTR), QTR)], fs.at[k], fr.at[y], at_y(k))

    def full_came(o):
        yt = (y + o) % NY
        return remote(kept.at[yt], full.at[pl.ds(pl.multiple_of(yt * QTR, QTR), QTR)], fs.at[yt], fr.at[yt], at_y(yt))

    def act_block(g):
        return act_t.at[:, pl.ds(pl.multiple_of(g * TOK, TOK), TOK)]

    def act_far():
        return remote(act_block(gy), act_block(gy), as_.at[0], ar.at[gy], far)

    def act_far_came():
        b = act_block(y * 2 + 1 - zh)
        return remote(b, b, as_.at[0], ar.at[y * 2 + 1 - zh], far)

    def act_copy(own, o):
        g = gy if own else y * 2 + 1 - zh
        return remote(act_block(g), act_block(g), as_.at[o + (0 if own else 3)], ar.at[g], at_y((y + o) % NY))

    def act_came(own, o):
        g = ((y + o) % NY) * 2 + (zh if own else 1 - zh)
        return remote(act_block(g), act_block(g), as_.at[o], ar.at[g], at_y((y + o) % NY))

    barrier = pltpu.get_barrier_semaphore()

    def greet(to):
        pl.semaphore_signal(barrier, inc=1, device_id=to, device_id_type=MESH)

    @pl.when(z > 0)
    def _():
        greet(at_z(z - 1))

    @pl.when(z < NZ - 1)
    def _():
        greet(at_z(z + 1))

    for to in (at_x(1), at_x(-1), twin, at_y((y + 1) % NY), at_y((y + 2) % NY), at_y((y + 3) % NY), far):
        greet(to)

    w_copy = pltpu.make_async_copy(w_hbm, w_ref, w_sem)
    w_copy.start()
    rows_all[pl.ds(pl.multiple_of(((z * NX + x) * 2 + c) * BLK, BLK), BLK), :] = g_ref[...]
    pl.semaphore_wait(barrier, 7 + (z > 0).astype(jnp.int32) + (z < NZ - 1).astype(jnp.int32))

    def spread(j):
        x_copy(j, 1).start()
        x_copy(j, 0).start()
        c_copy(j, 0).start()

    @pl.when(z < NZ - 1)
    def _():
        z_copy(z, 1).start()

    @pl.when(z > 0)
    def _():
        z_copy(z, 0).start()

    spread(z)

    hv = h_ref[...].astype(jnp.float32)
    tv = jnp.tanh(coeff * (hv + 0.044715 * hv * hv * hv))
    slope[...] = 0.5 * (1.0 + tv) + 0.5 * hv * (1.0 - tv * tv) * coeff * (1.0 + 3.0 * 0.044715 * hv * hv)
    act = 0.5 * hv * (1.0 + tv)
    act_t[:, pl.ds(pl.multiple_of(gy * TOK, TOK), TOK)] = act.T.astype(jnp.bfloat16)
    for o in (1, 2, 3):
        act_copy(True, o).start()
    w_copy.wait()

    def place(d, side):
        j = jnp.where(side == 0, z - d, z + d)
        valid = (d >= 0) & (d < NZ) & (j >= 0) & (j < NZ) & ((d > 0) | (side == 0))
        return j, valid

    def step(t, carry):
        for side in (0, 1):
            j, valid = place(t, side)

            @pl.when(valid)
            def _():
                z_copy(j, 1).wait_recv()

                @pl.when((z < NZ - 1) if side == 0 else (z > 0))
                def _():
                    z_copy(j, 1 - side).start()

                spread(j)

        @pl.when(t == ACT_SEND)
        def _():
            act_far().start()

        for side in (0, 1):
            j, valid = place(t - 1, side)

            @pl.when(valid)
            def _():
                x_came(j, 1).wait_recv()
                half_copy(j, 1).start()
                c_copy(j, 3).start()
                x_came(j, 0).wait_recv()
                half_copy(j, 0).start()
                c_copy(j, 1).start()

        for side in (0, 1):
            j, valid = place(t - 2, side)

            @pl.when(valid)
            def _():
                half_came(j, 1).wait_recv()
                half_came(j, 0).wait_recv()
                c_copy(j, 2).start()

        def multiply(side, carry):
            j, valid = place(t - 3, side)

            @pl.when(valid)
            def _():
                for o in range(NX):
                    c_came(j, o).wait_recv()
                part[j] = lax.dot_general(
                    rows_all[pl.ds(pl.multiple_of(j * TOK, TOK), TOK), :], w_ref[...],
                    (((1,), (1,)), ((), ())), preferred_element_type=jnp.float32)
                for o in (1, 2, 3):
                    y_copy(j, o).start()

            return carry

        lax.fori_loop(0, 2, multiply, 0)

        def add(side, carry):
            j, valid = place(t - 5, side)

            @pl.when(valid)
            def _():
                for o in (1, 2, 3):
                    y_copy(j, o).wait_recv()
                total = part[j, pl.ds(pl.multiple_of(y * QTR, QTR), QTR), :]
                total = total + from_y[0, j] + from_y[1, j] + from_y[2, j]
                k = j // 2

                @pl.when(j % 2 == zh)
                def _():
                    kept[k] = total

                @pl.when(j % 2 != zh)
                def _():
                    z_out[k] = total.astype(jnp.bfloat16)
                    far_copy(k).start()

            return carry

        lax.fori_loop(0, 2, add, 0)

        @pl.when(t == ACT_PASS)
        def _():
            act_far_came().wait_recv()
            for o in (1, 2, 3):
                act_copy(False, o).start()

        return carry

    lax.fori_loop(1, LAST, step, 0)

    for o in (1, 2, 3):
        act_came(True, o).wait_recv()
    for o in (1, 2, 3):
        act_came(False, o).wait_recv()

    def dw_copy(n):
        cols = pl.ds(pl.multiple_of(n * TILE, TILE), TILE)
        return pltpu.make_async_copy(dw_buf.at[:, cols], dw_hbm.at[:, cols], dw_sem.at[n])

    def weight_tile(n, carry):
        cols = pl.ds(pl.multiple_of(n * TILE, TILE), TILE)
        dw_buf[:, cols] = jnp.dot(act_t[...], rows_all[:, cols], preferred_element_type=jnp.float32)
        dw_copy(n).start()
        return carry

    lax.fori_loop(0, NT, weight_tile, 0)

    def finish(d, carry):
        for side in (0, 1):
            j, valid = place(d, side)

            @pl.when(valid & (j % 2 == zh))
            def _():
                k = j // 2
                far_copy(k).wait_recv()
                total = kept[k] + z_in[k].astype(jnp.float32)

                @pl.when(k == y)
                def _():
                    full[pl.ds(pl.multiple_of(y * QTR, QTR), QTR), :] = total

                @pl.when(k != y)
                def _():
                    kept[k] = total
                    full_copy(k).start()

        return carry

    lax.fori_loop(0, NZ, finish, 0)
    for o in (1, 2, 3):
        full_came(o).wait_recv()
    gh_ref[...] = (full[...] * slope[...]).astype(jnp.bfloat16)

    def sent(j, carry):
        @pl.when((z < NZ - 1) & (j <= z))
        def _():
            z_copy(j, 1).wait_send()

        @pl.when((z > 0) & (j >= z))
        def _():
            z_copy(j, 0).wait_send()

        for up in (0, 1):
            x_copy(j, up).wait_send()
            half_copy(j, up).wait_send()
        for o in range(NX):
            c_copy(j, o).wait_send()
        for o in (1, 2, 3):
            y_copy(j, o).wait_send()
        return carry

    lax.fori_loop(0, NZ, sent, 0)
    act_far().wait_send()
    for o in (1, 2, 3):
        act_copy(True, o).wait_send()
        act_copy(False, o).wait_send()

    def sent_sums(k, carry):
        far_copy(k).wait_send()

        @pl.when(k != y)
        def _():
            full_copy(k).wait_send()

        return carry

    lax.fori_loop(0, NY, sent_sums, 0)

    def stored(n, carry):
        dw_copy(n).wait()
        return carry

    lax.fori_loop(0, NT, stored, 0)


def body(hidden_pre, grad_out, down_weight):
    vmem = pl.BlockSpec(memory_space=pltpu.VMEM)
    hbm = pl.BlockSpec(memory_space=pl.ANY)
    dma = pltpu.SemaphoreType.DMA
    return pl.pallas_call(
        kernel,
        name="ffn_backward",
        out_shape=(jax.ShapeDtypeStruct((TOK, HID), jnp.bfloat16), jax.ShapeDtypeStruct((HID, FEAT), jnp.float32)),
        in_specs=[vmem, vmem, hbm],
        out_specs=(vmem, hbm),
        scratch_shapes=[
            pltpu.VMEM((NZ * TOK, FEAT), jnp.bfloat16),
            pltpu.VMEM((HID, FEAT), jnp.bfloat16),
            pltpu.VMEM((HID, NZ * TOK), jnp.bfloat16),
            pltpu.VMEM((TOK, HID), jnp.float32),
            pltpu.VMEM((NZ, TOK, HID), jnp.float32),
            pltpu.VMEM((NY - 1, NZ, QTR, HID), jnp.float32),
            pltpu.VMEM((NY, QTR, HID), jnp.float32),
            pltpu.VMEM((NY, QTR, HID), jnp.bfloat16),
            pltpu.VMEM((NY, QTR, HID), jnp.bfloat16),
            pltpu.VMEM((TOK, HID), jnp.float32),
            pltpu.VMEM((HID, FEAT), jnp.float32),
            dma, dma((NT,)),
            dma((2, NZ)), dma((NZ,)),
            dma((2, NZ)), dma((2, NZ)),
            dma((2, NZ)), dma((2, NZ)),
            dma((NX, NZ)), dma((NX, NZ)),
            dma((NY - 1, NZ)), dma((NY - 1, NZ)),
            dma((NY,)), dma((NY,)),
            dma((7,)), dma((NZ,)),
            dma((NY,)), dma((NY,)),
        ],
        compiler_params=pltpu.CompilerParams(
            collective_id=0, has_side_effects=True, vmem_limit_bytes=48 * 1024 * 1024),
        cost_estimate=pl.CostEstimate(flops=4 * 2048 * 1536 * 384, bytes_accessed=12 << 20, transcendentals=256 * 384),
    )(hidden_pre, grad_out, down_weight)


def solution(mesh):
    placed = (P("gy", ("gz", "gx")), P(("gx", "gz"), "gy"), P(("gz", "gx"), "gy"))
    return jax.shard_map(
        body,
        mesh=mesh,
        in_specs=placed,
        out_specs=(P("gy", ("gz", "gx")), P(("gz", "gx"), "gy")),
        check_vma=False,
    )
```

time: 436 us -> 107 us (0.25)
  waiting for transfers between devices: 404 us -> 0 us
  Pallas kernels: 0 us -> 99.4 us
  matrix products: 15.3 us -> 0 us
  between operations: 13.8 us -> 0.65 us
  local copies, waits for them, and re-layouts: 0.01 us -> 5.17 us
    all_gather x2 -> x0, waiting for transfers between devices: 232 us -> none  [the longest x1 134 us: body(): rows_all = lax.all_gather(grad_out, ('gx', 'gz'), axis=0, tiled=True)]
    reduce_scatter x1 -> x0, waiting for transfers between devices: 172 us -> none  [body(): lax.psum_scatter(against_weight(rows_all, down_weight), 'gy', scatter_dim...]
    pallas_call x0 -> x1, Pallas kernels: none -> 99.4 us  [body(): pl.pallas_call(kernel, name='ffn_backward', out_shape=(jax.ShapeDtypeStru...]
    dot_general x2 -> x0, matrix products: 15.3 us -> none  [the longest x1 7.94 us: against_weight(): lax.dot_general(rows, down_weight, (((1,), (1,)), ((), ())), preferred_el...]
    unnamed x4 -> x8, local copies, waits for them, and re-layouts: 0.01 us -> 5.17 us
  transfers between devices with their start and end apart: 3 -> 0, of which waited for: 3 -> 0; matrix products, arithmetic and copies ran while one was open for 0% -> 0% of each run, Pallas kernels for 0% -> 0%
where the time goes in v1:
time: 107 us; the launch traced here: 105 us
  Pallas kernels  99.4 us (93%)
  local copies, waits for them, and re-layouts  5.17 us (5%)
    pallas_call x1, Pallas kernels, body(): pl.pallas_call(kernel, name='ffn_backward', out_shape=(jax.ShapeDtypeStru...  99.4 us
    unnamed x8, local copies, waits for them, and re-layouts  5.17 us

profile of v1, /device:TPU:1, one launch (start us, length us, event | category | flops | bytes accessed | tf_op | source)
XLA Modules:
  0.0 105.2 jit_solution(18096371520776309945)
XLA Ops:
  0.6 0.0 copy-start
  0.6 1.3 %copy-done = bf16[384,1536]{1,0:T(8,128)(2,1)S(1)} copy-done((bf16[384,1536]{1,0:T(8,128)(2,1)S(1)}, bf16[384,1536]{1,0:T(8,128)(2,1)}, u32[]{:S(2)}) %copy-start) | copy-done | bytes 1179672
  1.9 0.0 copy-start.1
  1.9 0.9 copy-done.1
  2.8 0.0 copy-start.2
  2.8 0.9 copy-done.2
  3.7 99.4 %ffn_backward.1 = (bf16[256,384]{1,0:T(8,128)(2,1)S(1)}, f32[384,1536]{1,0:T(8,128)S(1)}) custom-call(bf16[256,384]{1,0:T(8,128)(2,1)S(1)} %copy-done.1, bf16[32,1536]{1,0:T(8,128)(2,1)S(1)} %copy-done.2, bf16[384,1536]{1,0:T(8,128)(2,1)S(1)} %copy-done), custom_call_target="tpu_custom_call" | custom-call | flops 4831838208 | bytes 12582912 | tf_op jit(solution)/shard_map/ffn_backward/pallas_call | solution.py:342
  103.2 0.7 copy.7
  103.8 1.4 %copy.8 = f32[384,1536]{1,0:T(8,128)} copy(f32[384,1536]{1,0:T(8,128)S(1)} %get-tuple-element.5) | data formatting | bytes 4718592
Async XLA Ops:
  0.6 1.3 %copy-start = (bf16[384,1536]{1,0:T(8,128)(2,1)S(1)}, bf16[384,1536]{1,0:T(8,128)(2,1)}, u32[]{:S(2)}) copy-start(bf16[384,1536]{1,0:T(8,128)(2,1)} %w_hbm.1) | copy-start | bytes 3538948
  1.9 0.9 copy-start.1
  2.8 0.9 copy-start.2

commit v2 on v1

v2 whole, which is shorter than its diff:
```python
import math

import jax
import jax.numpy as jnp
from jax import lax
from jax.experimental import pallas as pl
from jax.experimental.pallas import tpu as pltpu
from jax.sharding import PartitionSpec as P

MESH = pl.DeviceIdType.MESH
coeff = math.sqrt(2.0 / math.pi)

NZ, NY, NX = 8, 4, 4
BLK = 32
TOK = 256
QTR = TOK // NY
FEAT = 1536
HID = 384
TILE = 256
NT = FEAT // TILE
PARTS = 4
PIECE = HID // PARTS
ACT_SEND, ACT_PASS = 0, 4
LAG_MUL, LAG_ADD = 3, 5
LAST = 13
NAME = "ffn_backward"
Y_TYPE = jnp.bfloat16
VMEM_MB = 60
ORDER = [(p % NX) * 2 + p // NX for p in range(8)]


def kernel(h_hbm, g_hbm, w_hbm, gh_ref, dw_hbm,
           rows_all, h_ref, h_part, w_ref, act_t, product, part, mine, from_y, kept, z_out, z_in, own, full, dw_buf,
           in_sem, dw_sem, zs, zr, xs, xr, hs, hr, cs, cr, ys, yr, ts, tr, as_, ar, aos, aor, aps, apr, fs, fr, hqs, hqr):
    gx, gy, gz = lax.axis_index("gx"), lax.axis_index("gy"), lax.axis_index("gz")
    y, zh = gy // 2, gy % 2
    x, c = gz // 2, gz % 2
    z = gx

    def at_z(v):
        return {"gx": v, "gy": gy, "gz": gz}

    def at_x(o):
        return {"gx": gx, "gy": gy, "gz": ((x + o) % NX) * 2 + c}

    def at_y(v):
        return {"gx": gx, "gy": v * 2 + zh, "gz": gz}

    twin = {"gx": gx, "gy": gy, "gz": x * 2 + (1 - c)}
    far = {"gx": gx, "gy": y * 2 + (1 - zh), "gz": gz}

    def block(j, xx, cc, start=0, size=BLK):
        return rows_all.at[pl.ds(pl.multiple_of(((j * 2 + cc) * NX + xx) * BLK + start, 16), size)]

    def remote(src, dst, send, recv, to):
        return pltpu.make_async_remote_copy(
            src_ref=src, dst_ref=dst, send_sem=send, recv_sem=recv, device_id=to, device_id_type=MESH)

    def z_copy(j, up, half):
        b = block(j, x, c, half * 16, 16)
        return remote(b, b, zs.at[up, j, half], zr.at[j, half], at_z(z + 1 if up else z - 1))

    def x_copy(j, up):
        b = block(j, x, c)
        return remote(b, b, xs.at[up, j], xr.at[up, j], at_x(1 if up else -1))

    def x_came(j, up):
        b = block(j, (x + (NX - 1 if up else 1)) % NX, c)
        return remote(b, b, xs.at[up, j], xr.at[up, j], at_x(1 if up else -1))

    def half_copy(j, up):
        b = block(j, (x + (NX - 1 if up else 1)) % NX, c, 0 if up else 16, 16)
        return remote(b, b, hs.at[up, j], hr.at[up, j], at_x(1 if up else -1))

    def half_came(j, up):
        b = block(j, (x + 2) % NX, c, 0 if up else 16, 16)
        return remote(b, b, hs.at[up, j], hr.at[up, j], at_x(1 if up else -1))

    def half_of_place(j, cc):
        return rows_all.at[pl.ds(pl.multiple_of((j * 2 + cc) * NX * BLK, NX * BLK), NX * BLK)]

    def c_copy(j):
        b = half_of_place(j, c)
        return remote(b, b, cs.at[j], cr.at[j], twin)

    def c_came(j):
        b = half_of_place(j, 1 - c)
        return remote(b, b, cs.at[j], cr.at[j], twin)

    def y_copy(j, o):
        yt = (y + o) % NY
        return remote(part.at[j, pl.ds(pl.multiple_of(yt * QTR, QTR), QTR)], from_y.at[o - 1, j],
                      ys.at[o - 1, j], yr.at[o - 1, j], at_y(yt))

    def far_copy(k):
        return remote(z_out.at[k], z_in.at[k], ts.at[k], tr.at[k], far)

    def full_copy(k):
        return remote(own.at[k], full.at[pl.ds(pl.multiple_of(y * QTR, QTR), QTR)], fs.at[k], fr.at[y], at_y(k))

    def full_came(o):
        yt = (y + o) % NY
        return remote(own.at[yt], full.at[pl.ds(pl.multiple_of(yt * QTR, QTR), QTR)], fs.at[yt], fr.at[yt], at_y(yt))

    def h_copy_to(o):
        yt = (y + o) % NY
        return remote(h_ref.at[pl.ds(pl.multiple_of(yt * QTR, QTR), QTR)], h_part.at[y], hqs.at[o - 1], hqr.at[o - 1], at_y(yt))

    def h_came(o):
        return remote(h_part.at[y], h_part.at[(y + NY - o) % NY], hqs.at[o - 1], hqr.at[o - 1], at_y((y + o) % NY))

    def act_block(g, q=None):
        rows = pl.ds(0, HID) if q is None else pl.ds(q * PIECE, PIECE)
        return act_t.at[rows, pl.ds(pl.multiple_of(g * TOK, TOK), TOK)]

    other = y * 2 + 1 - zh

    def act_far(q):
        return remote(act_block(gy, q), act_block(gy, q), as_.at[q], ar.at[q], far)

    def act_far_came(q):
        return remote(act_block(other, q), act_block(other, q), as_.at[q], ar.at[q], far)

    def act_copy(o):
        return remote(act_block(gy), act_block(gy), aos.at[o - 1], aor.at[o - 1], at_y((y + o) % NY))

    def act_came(o):
        b = act_block(((y + NY - o) % NY) * 2 + zh)
        return remote(b, b, aos.at[o - 1], aor.at[o - 1], at_y((y + o) % NY))

    def act_pass(o, q):
        return remote(act_block(other, q), act_block(other, q), aps.at[o - 1, q], apr.at[o - 1, q], at_y((y + o) % NY))

    def act_passed(o, q):
        b = act_block(((y + NY - o) % NY) * 2 + 1 - zh, q)
        return remote(b, b, aps.at[o - 1, q], apr.at[o - 1, q], at_y((y + o) % NY))

    barrier = pltpu.get_barrier_semaphore()

    def greet(to):
        pl.semaphore_signal(barrier, inc=1, device_id=to, device_id_type=MESH)

    @pl.when(z > 0)
    def _():
        greet(at_z(z - 1))

    @pl.when(z < NZ - 1)
    def _():
        greet(at_z(z + 1))

    for to in (at_x(1), at_x(-1), twin, at_y((y + 1) % NY), at_y((y + 2) % NY), at_y((y + 3) % NY), far):
        greet(to)

    g_copy = pltpu.make_async_copy(g_hbm, block(z, x, c), in_sem.at[0])
    h_copies = [pltpu.make_async_copy(h_hbm.at[pl.ds(q * BLK, BLK)], h_ref.at[pl.ds(p * BLK, BLK)], in_sem.at[2 + p])
                for p, q in enumerate(ORDER)]
    w_copy = pltpu.make_async_copy(w_hbm, w_ref, in_sem.at[1])
    g_copy.start()
    for h_copy in h_copies:
        h_copy.start()
    w_copy.start()
    g_copy.wait()
    pl.semaphore_wait(barrier, 7 + (z > 0).astype(jnp.int32) + (z < NZ - 1).astype(jnp.int32))

    def spread(j):
        x_copy(j, 1).start()
        x_copy(j, 0).start()

    for half in (0, 1):
        @pl.when(z < NZ - 1)
        def _():
            z_copy(z, 1, half).start()

        @pl.when(z > 0)
        def _():
            z_copy(z, 0, half).start()

    spread(z)

    for h_copy in h_copies:
        h_copy.wait()
    for o in (1, 2, 3):
        h_copy_to(o).start()
    h_part[y] = h_ref[pl.ds(pl.multiple_of(y * QTR, QTR), QTR), :]
    hv = h_ref[...].astype(jnp.float32)
    act = 0.5 * hv * (1.0 + jnp.tanh(coeff * (hv + 0.044715 * hv * hv * hv)))
    act_t[:, pl.ds(pl.multiple_of(gy * TOK, TOK), TOK)] = act.T.astype(jnp.bfloat16)
    for o in (1, 2, 3):
        act_copy(o).start()
    for q in range(PARTS):
        if ACT_SEND + q <= 0:
            act_far(q).start()
    w_copy.wait()

    def place(d, side):
        j = jnp.where(side == 0, z - d, z + d)
        valid = (d >= 0) & (d < NZ) & (j >= 0) & (j < NZ) & ((d > 0) | (side == 0))
        return j, valid

    def step(t, carry):
        for half in (0, 1):
            for side in (0, 1):
                j, valid = place(t, side)

                @pl.when(valid)
                def _():
                    z_copy(j, 1, half).wait_recv()

                    @pl.when((z < NZ - 1) if side == 0 else (z > 0))
                    def _():
                        z_copy(j, 1 - side, half).start()

        for side in (0, 1):
            j, valid = place(t, side)

            @pl.when(valid)
            def _():
                spread(j)

        for q in range(PARTS):
            if ACT_SEND + q > 0:
                @pl.when(t == ACT_SEND + q)
                def _():
                    act_far(q).start()

        for side in (0, 1):
            j, valid = place(t - 1, side)

            @pl.when(valid)
            def _():
                x_came(j, 1).wait_recv()
                half_copy(j, 1).start()
                x_came(j, 0).wait_recv()
                half_copy(j, 0).start()

        for side in (0, 1):
            j, valid = place(t - 2, side)

            @pl.when(valid)
            def _():
                half_came(j, 1).wait_recv()
                half_came(j, 0).wait_recv()
                c_copy(j).start()

        def multiply(side, carry):
            j, valid = place(t - LAG_MUL, side)

            @pl.when(valid)
            def _():
                c_came(j).wait_recv()
                product[...] = lax.dot_general(
                    rows_all[pl.ds(pl.multiple_of(j * TOK, TOK), TOK), :], w_ref[...],
                    (((1,), (1,)), ((), ())), preferred_element_type=jnp.float32)
                part[j] = product[...].astype(part.dtype)
                mine[j] = product[pl.ds(pl.multiple_of(y * QTR, QTR), QTR), :]
                for o in (1, 2, 3):
                    y_copy(j, o).start()

            return carry

        lax.fori_loop(0, 2, multiply, 0)

        def add(side, carry):
            j, valid = place(t - LAG_ADD, side)

            @pl.when(valid)
            def _():
                for o in (1, 2, 3):
                    y_copy(j, o).wait_recv()
                total = mine[j]
                for o in (0, 1, 2):
                    total = total + from_y[o, j].astype(jnp.float32)
                k = j // 2

                @pl.when(j % 2 == zh)
                def _():
                    kept[k] = total

                @pl.when(j % 2 != zh)
                def _():
                    z_out[k] = total.astype(jnp.bfloat16)
                    far_copy(k).start()

            return carry

        lax.fori_loop(0, 2, add, 0)

        for q in range(PARTS):
            if ACT_PASS + q < LAST:
                @pl.when(t == ACT_PASS + q)
                def _():
                    act_far_came(q).wait_recv()
                    for o in (1, 2, 3):
                        act_pass(o, q).start()

        return carry

    lax.fori_loop(1, LAST, step, 0)

    def dw_copy(n):
        cols = pl.ds(pl.multiple_of(n * TILE, TILE), TILE)
        return pltpu.make_async_copy(dw_buf.at[:, cols], dw_hbm.at[:, cols], dw_sem.at[n])

    def weight_tile(n, carry):
        cols = pl.ds(pl.multiple_of(n * TILE, TILE), TILE)
        dw_buf[:, cols] = jnp.dot(act_t[...], rows_all[:, cols], preferred_element_type=jnp.float32)
        dw_copy(n).start()
        return carry


    def finish(d, carry):
        for side in (0, 1):
            j, valid = place(d, side)

            @pl.when(valid & (j % 2 == zh))
            def _():
                k = j // 2
                far_copy(k).wait_recv()
                grad_act = kept[k] + z_in[k].astype(jnp.float32)
                hk = h_part[k].astype(jnp.float32)
                tk = jnp.tanh(coeff * (hk + 0.044715 * hk * hk * hk))
                slope = 0.5 * (1.0 + tk) + 0.5 * hk * (1.0 - tk * tk) * coeff * (1.0 + 3.0 * 0.044715 * hk * hk)
                result = (grad_act * slope).astype(jnp.bfloat16)

                @pl.when(k == y)
                def _():
                    full[pl.ds(pl.multiple_of(y * QTR, QTR), QTR), :] = result

                @pl.when(k != y)
                def _():
                    own[k] = result
                    full_copy(k).start()

        return carry

    for o in (1, 2, 3):
        h_came(o).wait_recv()
    lax.fori_loop(0, NZ, finish, 0)

    for q in range(PARTS):
        if ACT_PASS + q >= LAST:
            act_far_came(q).wait_recv()
            for o in (1, 2, 3):
                act_pass(o, q).start()
    for o in (1, 2, 3):
        act_came(o).wait_recv()
        for q in range(PARTS):
            act_passed(o, q).wait_recv()

    lax.fori_loop(0, NT, weight_tile, 0)

    def sent(j, carry):
        for half in (0, 1):
            @pl.when((z < NZ - 1) & (j <= z))
            def _():
                z_copy(j, 1, half).wait_send()

            @pl.when((z > 0) & (j >= z))
            def _():
                z_copy(j, 0, half).wait_send()

        for up in (0, 1):
            x_copy(j, up).wait_send()
            half_copy(j, up).wait_send()
        c_copy(j).wait_send()
        for o in (1, 2, 3):
            y_copy(j, o).wait_send()
        return carry

    lax.fori_loop(0, NZ, sent, 0)
    for q in range(PARTS):
        act_far(q).wait_send()
    for o in (1, 2, 3):
        act_copy(o).wait_send()
        for q in range(PARTS):
            act_pass(o, q).wait_send()

    for o in (1, 2, 3):
        h_copy_to(o).wait_send()

    def sent_sums(k, carry):
        far_copy(k).wait_send()

        @pl.when(k != y)
        def _():
            full_copy(k).wait_send()

        return carry

    lax.fori_loop(0, NY, sent_sums, 0)

    for o in (1, 2, 3):
        full_came(o).wait_recv()
    for p, q in enumerate(ORDER):
        rows = slice(p * BLK, (p + 1) * BLK)
        gh_ref[q * BLK:(q + 1) * BLK, :] = full[rows, :]

    def stored(n, carry):
        dw_copy(n).wait()
        return carry

    lax.fori_loop(0, NT, stored, 0)


def body(hidden_pre, grad_out, down_weight):
    vmem = pl.BlockSpec(memory_space=pltpu.VMEM)
    hbm = pl.BlockSpec(memory_space=pl.ANY)
    dma = pltpu.SemaphoreType.DMA
    return pl.pallas_call(
        kernel,
        name=NAME,
        out_shape=(pltpu.VMEM((TOK, HID), jnp.bfloat16), pltpu.VMEM((HID, FEAT), jnp.float32)),
        in_specs=[hbm, hbm, hbm],
        out_specs=(vmem, hbm),
        scratch_shapes=[
            pltpu.VMEM((NZ * TOK, FEAT), jnp.bfloat16),
            pltpu.VMEM((TOK, HID), jnp.bfloat16),
            pltpu.VMEM((NY, QTR, HID), jnp.bfloat16),
            pltpu.VMEM((HID, FEAT), jnp.bfloat16),
            pltpu.VMEM((HID, NZ * TOK), jnp.bfloat16),
            pltpu.VMEM((TOK, HID), jnp.float32),
            pltpu.VMEM((NZ, TOK, HID), Y_TYPE),
            pltpu.VMEM((NZ, QTR, HID), jnp.float32),
            pltpu.VMEM((NY - 1, NZ, QTR, HID), Y_TYPE),
            pltpu.VMEM((NY, QTR, HID), jnp.float32),
            pltpu.VMEM((NY, QTR, HID), jnp.bfloat16),
            pltpu.VMEM((NY, QTR, HID), jnp.bfloat16),
            pltpu.VMEM((NY, QTR, HID), jnp.bfloat16),
            pltpu.VMEM((TOK, HID), jnp.bfloat16),
            pltpu.VMEM((HID, FEAT), jnp.float32),
            dma((10,)), dma((NT,)),
            dma((2, NZ, 2)), dma((NZ, 2)),
            dma((2, NZ)), dma((2, NZ)),
            dma((2, NZ)), dma((2, NZ)),
            dma((NZ,)), dma((NZ,)),
            dma((NY - 1, NZ)), dma((NY - 1, NZ)),
            dma((NY,)), dma((NY,)),
            dma((PARTS,)), dma((PARTS,)), dma((NY - 1,)), dma((NY - 1,)),
            dma((NY - 1, PARTS)), dma((NY - 1, PARTS)),
            dma((NY,)), dma((NY,)),
            dma((NY - 1,)), dma((NY - 1,)),
        ],
        compiler_params=pltpu.CompilerParams(
            collective_id=0, has_side_effects=True, vmem_limit_bytes=VMEM_MB * 1024 * 1024),
        cost_estimate=pl.CostEstimate(flops=4 * 2048 * 1536 * 384, bytes_accessed=12 << 20, transcendentals=256 * 384),
    )(hidden_pre, grad_out, down_weight)


def solution(mesh):
    placed = (P("gy", ("gz", "gx")), P(("gx", "gz"), "gy"), P(("gz", "gx"), "gy"))
    return jax.shard_map(
        body,
        mesh=mesh,
        in_specs=placed,
        out_specs=(P("gy", ("gz", "gx")), P(("gz", "gx"), "gy")),
        check_vma=False,
    )
```

time: 107 us -> 83.6 us (0.78); the launches traced: 105 us -> 83.5 us
  Pallas kernels: 99.4 us -> 80.8 us
  local copies, waits for them, and re-layouts: 5.17 us -> 2.08 us
    pallas_call x1, Pallas kernels: 99.4 us -> 80.8 us  [body(): pl.pallas_call(kernel, name=NAME, out_shape=(pltpu.VMEM((TOK, HID), jnp.b...]
    unnamed x8 -> x2, local copies, waits for them, and re-layouts: 5.17 us -> 2.08 us
where the time goes in v2:
time: 83.6 us; the launch traced here: 83.5 us
  Pallas kernels  80.8 us (97%)
  local copies, waits for them, and re-layouts  2.08 us (2%)
    pallas_call x1, Pallas kernels, body(): pl.pallas_call(kernel, name=NAME, out_shape=(pltpu.VMEM((TOK, HID), jnp.b...  80.8 us
    unnamed x2, local copies, waits for them, and re-layouts  2.08 us

profile of v2, /device:TPU:1, one launch (start us, length us, event | category | flops | bytes accessed | tf_op | source)
XLA Modules:
  0.0 83.5 jit_solution(16957364318340536479)
XLA Ops:
  0.6 80.8 %ffn_backward.1 = (bf16[256,384]{1,0:T(8,128)(2,1)S(1)}, f32[384,1536]{1,0:T(8,128)S(1)}) custom-call(bf16[256,384]{1,0:T(8,128)(2,1)} %h_hbm.1, bf16[32,1536]{1,0:T(8,128)(2,1)} %g_hbm.1, bf16[384,1536]{1,0:T(8,128)(2,1)} %w_hbm.1), custom_call_target="tpu_custom_call" | custom-call | flops 4831838208 | bytes 12582912 | tf_op jit(solution)/shard_map/ffn_backward/pallas_call | solution.py:409
  81.4 0.7 copy.7
  82.1 1.4 %copy.8 = f32[384,1536]{1,0:T(8,128)} copy(f32[384,1536]{1,0:T(8,128)S(1)} %get-tuple-element.3) | data formatting | bytes 4718592

commit v3 on v2

--- a/solution.py
+++ b/solution.py
@@ -20,8 +20,8 @@
 NT = FEAT // TILE
 PARTS = 4
 PIECE = HID // PARTS
-ACT_SEND, ACT_PASS = 0, 4
-LAG_MUL, LAG_ADD = 3, 5
+ACT_SEND, ACT_PASS = (0, 1), 4
+LAG_X, LAG_HALF, LAG_MUL, LAG_ADD = 1, 2, 3, 5
 LAST = 13
 NAME = "ffn_backward"
 Y_TYPE = jnp.bfloat16
@@ -60,13 +60,13 @@
         b = block(j, x, c, half * 16, 16)
         return remote(b, b, zs.at[up, j, half], zr.at[j, half], at_z(z + 1 if up else z - 1))
 
-    def x_copy(j, up):
-        b = block(j, x, c)
-        return remote(b, b, xs.at[up, j], xr.at[up, j], at_x(1 if up else -1))
-
-    def x_came(j, up):
-        b = block(j, (x + (NX - 1 if up else 1)) % NX, c)
-        return remote(b, b, xs.at[up, j], xr.at[up, j], at_x(1 if up else -1))
+    def x_copy(j, up, half):
+        b = block(j, x, c, half * 16, 16)
+        return remote(b, b, xs.at[up, j, half], xr.at[up, j, half], at_x(1 if up else -1))
+
+    def x_came(j, up, half):
+        b = block(j, (x + (NX - 1 if up else 1)) % NX, c, half * 16, 16)
+        return remote(b, b, xs.at[up, j, half], xr.at[up, j, half], at_x(1 if up else -1))
 
     def half_copy(j, up):
         b = block(j, (x + (NX - 1 if up else 1)) % NX, c, 0 if up else 16, 16)
@@ -163,8 +163,10 @@
     pl.semaphore_wait(barrier, 7 + (z > 0).astype(jnp.int32) + (z < NZ - 1).astype(jnp.int32))
 
     def spread(j):
-        x_copy(j, 1).start()
-        x_copy(j, 0).start()
+        x_copy(j, 1, 0).start()
+        x_copy(j, 0, 1).start()
+        x_copy(j, 1, 1).start()
+        x_copy(j, 0, 0).start()
 
     for half in (0, 1):
         @pl.when(z < NZ - 1)
@@ -187,8 +189,10 @@
     act_t[:, pl.ds(pl.multiple_of(gy * TOK, TOK), TOK)] = act.T.astype(jnp.bfloat16)
     for o in (1, 2, 3):
         act_copy(o).start()
+    act_send = jnp.where(zh == 0, ACT_SEND[0], ACT_SEND[1])
     for q in range(PARTS):
-        if ACT_SEND + q <= 0:
+        @pl.when(act_send + q <= 0)
+        def _():
             act_far(q).start()
     w_copy.wait()
 
@@ -218,26 +222,27 @@
                 spread(j)
 
         for q in range(PARTS):
-            if ACT_SEND + q > 0:
-                @pl.when(t == ACT_SEND + q)
-                def _():
-                    act_far(q).start()
+            @pl.when(t == act_send + q)
+            def _():
+                act_far(q).start()
 
         for side in (0, 1):
-            j, valid = place(t - 1, side)
+            j, valid = place(t - LAG_X, side)
 
             @pl.when(valid)
             def _():
-                x_came(j, 1).wait_recv()
+                x_came(j, 1, 0).wait_recv()
                 half_copy(j, 1).start()
-                x_came(j, 0).wait_recv()
+                x_came(j, 0, 1).wait_recv()
                 half_copy(j, 0).start()
 
         for side in (0, 1):
-            j, valid = place(t - 2, side)
+            j, valid = place(t - LAG_HALF, side)
 
             @pl.when(valid)
             def _():
+                x_came(j, 1, 1).wait_recv()
+                x_came(j, 0, 0).wait_recv()
                 half_came(j, 1).wait_recv()
                 half_came(j, 0).wait_recv()
                 c_copy(j).start()
@@ -286,12 +291,11 @@
         lax.fori_loop(0, 2, add, 0)
 
         for q in range(PARTS):
-            if ACT_PASS + q < LAST:
-                @pl.when(t == ACT_PASS + q)
-                def _():
-                    act_far_came(q).wait_recv()
-                    for o in (1, 2, 3):
-                        act_pass(o, q).start()
+            @pl.when(t == ACT_PASS + q)
+            def _():
+                act_far_came(q).wait_recv()
+                for o in (1, 2, 3):
+                    act_pass(o, q).start()
 
         return carry
 
@@ -335,18 +339,12 @@
 
     for o in (1, 2, 3):
         h_came(o).wait_recv()
+        act_came(o).wait_recv()
+
     lax.fori_loop(0, NZ, finish, 0)
-
-    for q in range(PARTS):
-        if ACT_PASS + q >= LAST:
-            act_far_came(q).wait_recv()
-            for o in (1, 2, 3):
-                act_pass(o, q).start()
-    for o in (1, 2, 3):
-        act_came(o).wait_recv()
+    for o in (1, 2, 3):
         for q in range(PARTS):
             act_passed(o, q).wait_recv()
-
     lax.fori_loop(0, NT, weight_tile, 0)
 
     def sent(j, carry):
@@ -360,7 +358,8 @@
                 z_copy(j, 0, half).wait_send()
 
         for up in (0, 1):
-            x_copy(j, up).wait_send()
+            x_copy(j, up, 0).wait_send()
+            x_copy(j, up, 1).wait_send()
             half_copy(j, up).wait_send()
         c_copy(j).wait_send()
         for o in (1, 2, 3):
@@ -430,7 +429,7 @@
             pltpu.VMEM((HID, FEAT), jnp.float32),
             dma((10,)), dma((NT,)),
             dma((2, NZ, 2)), dma((NZ, 2)),
-            dma((2, NZ)), dma((2, NZ)),
+            dma((2, NZ, 2)), dma((2, NZ, 2)),
             dma((2, NZ)), dma((2, NZ)),
             dma((NZ,)), dma((NZ,)),
             dma((NY - 1, NZ)), dma((NY - 1, NZ)),

time: 83.6 us -> 81.7 us (0.977)
  Pallas kernels: 80.8 us -> 78.9 us
    pallas_call x1, Pallas kernels: 80.8 us -> 78.9 us  [body(): pl.pallas_call(kernel, name=NAME, out_shape=(pltpu.VMEM((TOK, HID), jnp.b...]
where the time goes in v3:
time: 81.7 us; the launch traced here: 81.6 us
  Pallas kernels  78.9 us (97%)
  local copies, waits for them, and re-layouts  2.08 us (3%)
    pallas_call x1, Pallas kernels, body(): pl.pallas_call(kernel, name=NAME, out_shape=(pltpu.VMEM((TOK, HID), jnp.b...  78.9 us
    unnamed x2, local copies, waits for them, and re-layouts  2.08 us

profile of v3, /device:TPU:1, one launch (start us, length us, event | category | flops | bytes accessed | tf_op | source)
XLA Modules:
  0.0 81.6 jit_solution(17310139303619522466)
XLA Ops:
  0.6 78.9 %ffn_backward.1 = (bf16[256,384]{1,0:T(8,128)(2,1)S(1)}, f32[384,1536]{1,0:T(8,128)S(1)}) custom-call(bf16[256,384]{1,0:T(8,128)(2,1)} %h_hbm.1, bf16[32,1536]{1,0:T(8,128)(2,1)} %g_hbm.1, bf16[384,1536]{1,0:T(8,128)(2,1)} %w_hbm.1), custom_call_target="tpu_custom_call" | custom-call | flops 4831838208 | bytes 12582912 | tf_op jit(solution)/shard_map/ffn_backward/pallas_call | solution.py:408
  79.5 0.7 copy.7
  80.2 1.4 %copy.8 = f32[384,1536]{1,0:T(8,128)} copy(f32[384,1536]{1,0:T(8,128)S(1)} %get-tuple-element.3) | data formatting | bytes 4718592

commit v4 on v3

--- a/solution.py
+++ b/solution.py
@@ -21,10 +21,10 @@
 PARTS = 4
 PIECE = HID // PARTS
 ACT_SEND, ACT_PASS = (0, 1), 4
-LAG_X, LAG_HALF, LAG_MUL, LAG_ADD = 1, 2, 3, 5
-LAST = 13
+LAG_X, LAG_HALF, LAG_MUL, LAG_ADD = 1, 2, 3, 6
+LAST = 14
 NAME = "ffn_backward"
-Y_TYPE = jnp.bfloat16
+Y_TYPE = jnp.float32
 VMEM_MB = 60
 ORDER = [(p % NX) * 2 + p // NX for p in range(8)]
 

time: 81.7 us -> 93 us (1.14)
  the two profiles are of different devices: /device:TPU:1 before, /device:TPU:96 now
where the time goes in v4:
time: 93 us; the launch traced here: 92.9 us
  Pallas kernels  90.2 us (97%)
  local copies, waits for them, and re-layouts  2.08 us (2%)
    pallas_call x1, Pallas kernels, body(): pl.pallas_call(kernel, name=NAME, out_shape=(pltpu.VMEM((TOK, HID), jnp.b...  90.2 us
    unnamed x2, local copies, waits for them, and re-layouts  2.08 us

profile of v4, /device:TPU:96, one launch (start us, length us, event | category | flops | bytes accessed | tf_op | source)
XLA Modules:
  0.0 92.9 jit_solution(2314478010490456618)
XLA Ops:
  0.6 90.2 %ffn_backward.1 = (bf16[256,384]{1,0:T(8,128)(2,1)S(1)}, f32[384,1536]{1,0:T(8,128)S(1)}) custom-call(bf16[256,384]{1,0:T(8,128)(2,1)} %h_hbm.1, bf16[32,1536]{1,0:T(8,128)(2,1)} %g_hbm.1, bf16[384,1536]{1,0:T(8,128)(2,1)} %w_hbm.1), custom_call_target="tpu_custom_call" | custom-call | flops 4831838208 | bytes 12582912 | tf_op jit(solution)/shard_map/ffn_backward/pallas_call | solution.py:408
  90.8 0.7 copy.7
  91.5 1.4 %copy.8 = f32[384,1536]{1,0:T(8,128)} copy(f32[384,1536]{1,0:T(8,128)S(1)} %get-tuple-element.3) | data formatting | bytes 4718592

commit v5 on v3

--- a/solution.py
+++ b/solution.py
@@ -16,7 +16,7 @@
 QTR = TOK // NY
 FEAT = 1536
 HID = 384
-TILE = 256
+TILE = 512
 NT = FEAT // TILE
 PARTS = 4
 PIECE = HID // PARTS
@@ -29,9 +29,9 @@
 ORDER = [(p % NX) * 2 + p // NX for p in range(8)]
 
 
-def kernel(h_hbm, g_hbm, w_hbm, gh_ref, dw_hbm,
-           rows_all, h_ref, h_part, w_ref, act_t, product, part, mine, from_y, kept, z_out, z_in, own, full, dw_buf,
-           in_sem, dw_sem, zs, zr, xs, xr, hs, hr, cs, cr, ys, yr, ts, tr, as_, ar, aos, aor, aps, apr, fs, fr, hqs, hqr):
+def kernel(h_hbm, g_hbm, w_hbm, gh_ref, dw_ref,
+           rows_all, h_ref, h_part, w_ref, act_t, product, part, mine, from_y, kept, z_out, z_in, own, full,
+           in_sem, zs, zr, xs, xr, hs, hr, cs, cr, ys, yr, ts, tr, as_, ar, aos, aor, aps, apr, fs, fr, hqs, hqr):
     gx, gy, gz = lax.axis_index("gx"), lax.axis_index("gy"), lax.axis_index("gz")
     y, zh = gy // 2, gy % 2
     x, c = gz // 2, gz % 2
@@ -301,14 +301,9 @@
 
     lax.fori_loop(1, LAST, step, 0)
 
-    def dw_copy(n):
-        cols = pl.ds(pl.multiple_of(n * TILE, TILE), TILE)
-        return pltpu.make_async_copy(dw_buf.at[:, cols], dw_hbm.at[:, cols], dw_sem.at[n])
-
     def weight_tile(n, carry):
         cols = pl.ds(pl.multiple_of(n * TILE, TILE), TILE)
-        dw_buf[:, cols] = jnp.dot(act_t[...], rows_all[:, cols], preferred_element_type=jnp.float32)
-        dw_copy(n).start()
+        dw_ref[:, cols] = jnp.dot(act_t[...], rows_all[:, cols], preferred_element_type=jnp.float32)
         return carry
 
 
@@ -393,12 +388,6 @@
     for p, q in enumerate(ORDER):
         rows = slice(p * BLK, (p + 1) * BLK)
         gh_ref[q * BLK:(q + 1) * BLK, :] = full[rows, :]
-
-    def stored(n, carry):
-        dw_copy(n).wait()
-        return carry
-
-    lax.fori_loop(0, NT, stored, 0)
 
 
 def body(hidden_pre, grad_out, down_weight):
@@ -410,7 +399,7 @@
         name=NAME,
         out_shape=(pltpu.VMEM((TOK, HID), jnp.bfloat16), pltpu.VMEM((HID, FEAT), jnp.float32)),
         in_specs=[hbm, hbm, hbm],
-        out_specs=(vmem, hbm),
+        out_specs=(vmem, vmem),
         scratch_shapes=[
             pltpu.VMEM((NZ * TOK, FEAT), jnp.bfloat16),
             pltpu.VMEM((TOK, HID), jnp.bfloat16),
@@ -426,8 +415,7 @@
             pltpu.VMEM((NY, QTR, HID), jnp.bfloat16),
             pltpu.VMEM((NY, QTR, HID), jnp.bfloat16),
             pltpu.VMEM((TOK, HID), jnp.bfloat16),
-            pltpu.VMEM((HID, FEAT), jnp.float32),
-            dma((10,)), dma((NT,)),
+            dma((10,)),
             dma((2, NZ, 2)), dma((NZ, 2)),
             dma((2, NZ, 2)), dma((2, NZ, 2)),
             dma((2, NZ)), dma((2, NZ)),

time: 81.7 us -> 80.9 us (level)
  Pallas kernels: 78.9 us -> 78 us
where the time goes in v5:
time: 80.9 us; the launch traced here: 80.8 us
  Pallas kernels  78 us (96%)
  local copies, waits for them, and re-layouts  2.08 us (3%)
    pallas_call x1, Pallas kernels, body(): pl.pallas_call(kernel, name=NAME, out_shape=(pltpu.VMEM((TOK, HID), jnp.b...  78 us
    unnamed x2, local copies, waits for them, and re-layouts  2.08 us

profile of v5, /device:TPU:1, one launch (start us, length us, event | category | flops | bytes accessed | tf_op | source)
XLA Modules:
  0.0 80.8 jit_solution(12595242184146187506)
XLA Ops:
  0.6 78.0 %ffn_backward.1 = (bf16[256,384]{1,0:T(8,128)(2,1)S(1)}, f32[384,1536]{1,0:T(8,128)S(1)}) custom-call(bf16[256,384]{1,0:T(8,128)(2,1)} %h_hbm.1, bf16[32,1536]{1,0:T(8,128)(2,1)} %g_hbm.1, bf16[384,1536]{1,0:T(8,128)(2,1)} %w_hbm.1), custom_call_target="tpu_custom_call" | custom-call | flops 4831838208 | bytes 12582912 | tf_op jit(solution)/shard_map/ffn_backward/pallas_call | solution.py:397
  78.7 0.7 copy.7
  79.4 1.4 %copy.8 = f32[384,1536]{1,0:T(8,128)} copy(f32[384,1536]{1,0:T(8,128)S(1)} %get-tuple-element.3) | data formatting | bytes 4718592
